TPU v7x, 512 devices: a whole 4x4x16 slice. The times are simulated.
512 devices in a mesh: dp: 32 (over y_lo, z), tensor: 16 (over x, y_hi, core).
Axes of the slice: x: 4, y: 4 (y_hi: 2, y_lo: 2; y = y_hi * 2 + y_lo), z: 16, core: 2. Of those that a mesh axis runs over, the one named last changes fastest.
Arguments:
- hidden: bfloat16 [8192, 14336], P('dp', 'tensor'), may hold values from -6 to 6
- tenant_ids: int32 [16], replicated, may hold values from 0 to 3
- base_weight: bfloat16 [14336, 4096], P('tensor', 'dp'), may hold values from -0.09375 to 0.09375
- adapter_in: bfloat16 [14336, 128], P('tensor'), may hold values from -0.10857488 to 0.10857488
- adapter_out: bfloat16 [128, 4096], P(None, 'tensor'), may hold values from -0.5 to 0.5
- magnitude: float32 [4, 4096], P(None, 'tensor'), may hold values from 0.5 to 2
- cotangent: bfloat16 [8192, 4096], P('dp', 'tensor'), may hold values from -6 to 6
Outputs:
- adapted: bfloat16 [8192, 4096], P('dp', 'tensor')
- input_grad: bfloat16 [8192, 14336], P('dp', 'tensor')
- grad_in: float32 [14336, 128], P('tensor')
- grad_out: float32 [128, 4096], P(None, 'tensor')
- grad_mag: float32 [4, 4096], P(None, 'tensor')
Inputs may be any that keep to these rules, and one draw needn't show every extreme that they name: `tenant_ids`: the tenant of each block of 512 consecutive tokens.
All inputs are finite; a program needn't handle non-finite values.
Results may differ from a plain program's by a relative error of at most 0.0049.
Values may be sent and summed in bfloat16 or wider, within the bound.
A program may use at most 64 MiB of HBM per device.

v0:
```python
import jax
import jax.numpy as jnp
from jax import lax
from jax.sharding import PartitionSpec as P

BLOCK = 512


epsilon = 1e-06


def inner_rows(lhs_mat, rhs_mat, precision=None):
    return lax.dot_general(
        lhs_mat,
        rhs_mat,
        (((0,), (0,)), ((), ())),
        precision=precision,
        preferred_element_type=jnp.float32,
    )


def outer_rows(lhs_mat, rhs_mat, precision=None):
    return lax.dot_general(
        lhs_mat,
        rhs_mat,
        (((1,), (1,)), ((), ())),
        precision=precision,
        preferred_element_type=jnp.float32,
    )


def per_device(hidden, tenant_ids, base_weight, adapter_in, adapter_out, magnitude, cotangent):
    highest = lax.Precision.HIGHEST
    row_count = hidden.shape[0]
    adapt = adapter_in.shape[1]
    tenants = magnitude.shape[0]
    rank = adapt // tenants
    width_local = adapter_out.shape[1]
    row_ids = lax.axis_index("dp") * row_count + jnp.arange(row_count, dtype=jnp.int32)
    block_ids = row_ids // BLOCK
    block_hot = block_ids[:, None] == jnp.arange(tenant_ids.shape[0], dtype=jnp.int32)[None, :]
    tenant = jnp.sum(jnp.where(block_hot, tenant_ids[None, :], 0), axis=1)
    col_owner = jnp.arange(adapt, dtype=jnp.int32) // rank
    col_mask = (tenant[:, None] == col_owner[None, :]).astype(jnp.float32)
    onehot = (tenant[:, None] == jnp.arange(tenants, dtype=jnp.int32)[None, :]).astype(jnp.float32)
    column_start = lax.axis_index("tensor") * width_local
    out_rows = lax.all_gather(adapter_out, "tensor", axis=1, tiled=True)
    out_wide = out_rows.astype(jnp.float32)
    block_mask = (col_owner[:, None] == col_owner[None, :]).astype(jnp.float32)
    adapter_gram = inner_rows(adapter_in, adapter_in) * block_mask
    gathered = lax.all_gather(base_weight, "dp", axis=1, tiled=True)
    cross_term = inner_rows(adapter_in, gathered)
    inner_term = jnp.dot(adapter_gram, out_wide, precision=highest)
    per_tenant = ((2.0 * cross_term + inner_term) * out_wide).reshape(tenants, rank, -1).sum(axis=1)
    column_sq = jnp.sum(jnp.square(gathered.astype(jnp.float32)), axis=0)
    squares_all = lax.psum(per_tenant + column_sq[None, :], "tensor")
    squares = lax.dynamic_slice_in_dim(squares_all, column_start, width_local, 1)
    length = jnp.sqrt(squares + epsilon)
    col_scale = magnitude / length
    tok_scale = jnp.dot(onehot, col_scale, precision=highest)
    lowrank_part = jnp.dot(hidden, adapter_in, preferred_element_type=jnp.float32) * col_mask
    lowrank = lax.psum(lowrank_part, "tensor")
    base_part = jnp.dot(hidden, gathered, preferred_element_type=jnp.float32)
    summed = lax.psum_scatter(base_part, "tensor", scatter_dimension=1, tiled=True)
    summed = summed + jnp.dot(lowrank, adapter_out.astype(jnp.float32), precision=highest)
    adapted = (summed * tok_scale).astype(jnp.bfloat16)
    slopes = (cotangent.astype(jnp.float32) * tok_scale).astype(jnp.bfloat16)
    grad_out_part = inner_rows(lowrank, slopes.astype(jnp.float32), highest)
    grad_mag_part = inner_rows(onehot, cotangent.astype(jnp.float32) * summed, highest)
    sliced = lax.all_gather(slopes, "tensor", axis=1, tiled=True)
    back_base = outer_rows(sliced, gathered)
    back_wide = outer_rows(sliced, out_rows)
    back_adapt = back_wide * col_mask
    input_grad = (
        back_base + outer_rows(back_adapt, adapter_in.astype(jnp.float32), highest)
    ).astype(jnp.bfloat16)
    grad_in_part = inner_rows(hidden.astype(jnp.float32), back_adapt, highest)
    grad_in, grad_out, grad_mag_sum = lax.psum((grad_in_part, grad_out_part, grad_mag_part), "dp")
    grad_mag = grad_mag_sum / length
    return (adapted, input_grad, grad_in, grad_out, grad_mag)


def solution(mesh):
    return jax.shard_map(
        per_device,
        mesh=mesh,
        in_specs=(
            P("dp", "tensor"),
            P(),
            P("tensor", "dp"),
            P("tensor", None),
            P(None, "tensor"),
            P(None, "tensor"),
            P("dp", "tensor"),
        ),
        out_specs=(
            P("dp", "tensor"),
            P("dp", "tensor"),
            P("tensor", None),
            P(None, "tensor"),
            P(None, "tensor"),
        ),
        check_vma=False,
    )
```

profile of v0, /device:TPU:2, one launch (start us, length us, event | category | flops | bytes accessed | tf_op | source)
XLA Modules:
  0.0 833.3 jit_solution(16201834001555906867)
XLA Ops:
  8.0 0.7 all-gather.6.cloned.1.call-update
  8.7 0.7 select_reduce_fusion
  9.5 1.3 convolution_select_fusion.2
  10.8 1.9 convolution_select_fusion
  12.7 169.5 %all-gather.4.cloned.1.call-done = bf16[896,4096]{1,0:T(8,128)(2,1)} async-done(((bf16[896,128]{1,0:T(8,128)(2,1)}), bf16[896,4096]{1,0:T(8,128)(2,1)}) %all-gather.4.cloned.1.call-update) | async-done | bytes 7340048 | tf_op jit(solution)/shard_map/all_gather | solution.py:51
  182.2 4.6 convolution_multiply_fusion
  187.5 1.5 multiply_reduce_fusion
  189.0 52.2 %all-gather.6.cloned.1.call-done = bf16[128,4096]{1,0:T(8,128)(2,1)} async-done(((bf16[128,256]{1,0:T(8,128)(2,1)}), bf16[128,4096]{1,0:T(8,128)(2,1)}) %all-gather.6.cloned.1.call-update) | async-done | bytes 1048592 | tf_op jit(solution)/shard_map/all_gather | solution.py:47
  241.2 2.8 bitcast_reduce_fusion
  244.7 7.5 fusion.12
  252.3 137.2 %all-reduce.7.cloned.1.call-done = (f32[256,128]{1,0:T(8,128)}, f32[4,4096]{1,0:T(4,128)}) async-done(((f32[256,128]{1,0:T(8,128)}, f32[4,4096]{1,0:T(4,128)}), (f32[256,128]{1,0:T(8,128)}, f32[4,4096]{1,0:T(4,128)})) %all-reduce.7.cloned.1.call-update) | async-done | bytes 196624 | tf_op jit(solution)/shard_map/psum | solution.py:62
  389.6 109.8 %reduce-scatter.2.cloned.1.call-done = f32[256,256]{1,0:T(8,128)} async-done(((f32[256,4096]{1,0:T(8,128)}), f32[256,256]{1,0:T(8,128)}) %reduce-scatter.2.cloned.1.call-update) | async-done | bytes 262160 | tf_op jit(solution)/shard_map/reduce_scatter | solution.py:64
  499.4 1.3 convolution_add_fusion.2
  500.7 1.7 fusion.2
  502.8 64.3 %psum.39 = f32[4,256]{1,0:T(4,128)S(1)} all-reduce(f32[4,256]{1,0:T(4,128)S(1)} %fusion.3), channel_id=1, replica_groups=mesh['dp'=32,'tensor'=16] {'dp'}, use_global_device_ids=true, to_apply=%region_8.9 | all-reduce | flops 1024 | bytes 8192 | tf_op jit(solution)/shard_map/psum | solution.py:78
  567.1 1.3 fusion.8
  568.4 1.9 fusion.14
  570.3 2.3 convolution_select_fusion.1
  572.6 1.2 convolution_bitcast_fusion
  573.8 6.1 fusion.13
  579.9 1.3 fusion.1
  581.2 241.6 %all-reduce.5.cloned.1.call-done = (f32[896,128]{0,1:T(8,128)}, f32[128,256]{1,0:T(8,128)}) async-done(((f32[896,128]{0,1:T(8,128)}, f32[128,256]{1,0:T(8,128)}), (f32[896,128]{0,1:T(8,128)}, f32[128,256]{1,0:T(8,128)})) %all-reduce.5.cloned.1.call-update) | async-done | bytes 589840 | tf_op jit(solution)/shard_map/psum | solution.py:78
  822.9 2.0 copy.13
  824.8 1.6 copy.18
  (30 shorter events, 2.7 us)
Async XLA Ops:
  7.2 3.6 copy-start
  7.2 175.0 %all-gather.4.cloned.1.call-start = ((), (), s32[]{:S(2)}) async-start(), calls=%async_computation.1 | async-start | bytes 7569408 | tf_op jit(solution)/shard_map/all_gather | solution.py:51
  7.9 233.3 %all-gather.6.cloned.1.call-start = ((), (), s32[]{:S(2)}) async-start(), calls=%async_computation.3 | async-start | bytes 1114112 | tf_op jit(solution)/shard_map/all_gather | solution.py:47
  8.7 380.9 %all-reduce.7.cloned.1.call-start = ((), (), s32[]{:S(2)}) async-start(), calls=%async_computation.6 | async-start | bytes 393216 | tf_op jit(solution)/shard_map/psum | solution.py:62
  182.2 5.3 copy-start.1
  244.7 254.7 %reduce-scatter.2.cloned.1.call-start = ((), (), s32[]{:S(2)}) async-start(), calls=%async_computation.2 | async-start | bytes 4456448 | tf_op jit(solution)/shard_map/reduce_scatter | solution.py:64
  252.2 247.1 %copy-start.5 = (bf16[128,256]{1,0:T(8,128)(2,1)S(1)}, bf16[128,256]{1,0:T(8,128)(2,1)}, u32[]{:S(2)}) copy-start(bf16[128,256]{1,0:T(8,128)(2,1)} %param.11) | copy-start | bytes 196612
  252.2 248.4 %copy-start.4 = (bf16[256,256]{1,0:T(8,128)(2,1)S(1)}, bf16[256,256]{1,0:T(8,128)(2,1)}, u32[]{:S(2)}) copy-start(bf16[256,256]{1,0:T(8,128)(2,1)} %param.13) | copy-start | bytes 393220
  252.2 248.4 %copy-start.6 = (f32[4,256]{1,0:T(4,128)S(1)}, f32[4,256]{1,0:T(4,128)}, u32[]{:S(2)}) copy-start(f32[4,256]{1,0:T(4,128)} %param.12) | copy-start | bytes 12292
  252.3 318.0 %copy-start.3 = (bf16[128,4096]{1,0:T(8,128)(2,1)S(1)}, bf16[128,4096]{1,0:T(8,128)(2,1)}, u32[]{:S(2)}) copy-start(bf16[128,4096]{1,0:T(8,128)(2,1)} %all-gather.6.cloned.1.call-done) | copy-start | bytes 3145732
  252.3 318.0 %all-gather.8.cloned.1.call-start = ((), (), s32[]{:S(2)}) async-start(), calls=%async_computation.4 | async-start | bytes 2228224 | tf_op jit(solution)/shard_map/all_gather | solution.py:70
  502.4 320.5 %all-reduce.5.cloned.1.call-start = ((), (), s32[]{:S(2)}) async-start(), calls=%async_computation.5 | async-start | bytes 1179648 | tf_op jit(solution)/shard_map/psum | solution.py:78
  573.8 6.1 copy-start.2
Sparse Core Ops, SparseCore 0:
  10.0 172.1 all-gather.3
  185.3 55.7 all-gather.5
  244.8 144.7 all-reduce.6
  395.1 104.2 reduce-scatter.1
  502.9 63.9 all-gather.7
  573.9 248.9 all-reduce.4
where the time goes:
time: 834 us; the launch traced here: 833 us
  waiting for transfers between devices  712 us (85%)
  blocking collectives  64.3 us (8%)
  matrix products  34.2 us (4%)
  between operations  14.2 us (2%)
    psum x1, waiting for transfers between devices, per_device(): lax.psum((grad_in_part, grad_out_part, grad_mag_part), 'dp')  242 us
    all_gather x1, waiting for transfers between devices, per_device(): gathered = lax.all_gather(base_weight, 'dp', axis=1, tiled=True)  170 us
    psum x1, waiting for transfers between devices, per_device(): lowrank = lax.psum(lowrank_part, 'tensor')  137 us
    reduce_scatter x1, waiting for transfers between devices, per_device(): lax.psum_scatter(base_part, 'tensor', scatter_dimension=1, tiled=True)  110 us
    psum x1, blocking collectives, per_device(): lax.psum((grad_in_part, grad_out_part, grad_mag_part), 'dp')  64.3 us
    all_gather x1, waiting for transfers between devices, per_device(): out_rows = lax.all_gather(adapter_out, 'tensor', axis=1, tiled=True)  52.2 us
  transfers between devices with their start and end apart: 6, of which 5 were waited for; matrix products, arithmetic and copies ran while one was open for 3% of the time, Pallas kernels for 0%

commit v1 on v0

v1 whole, which is shorter than its diff:
```python
import functools

import jax
import jax.numpy as jnp
from jax import lax
from jax.experimental import pallas as pl
from jax.experimental.pallas import tpu as pltpu
from jax.sharding import PartitionSpec as P

epsilon = 1e-06
f32 = jnp.float32
bf16 = jnp.bfloat16
MESH = pl.DeviceIdType.MESH


def dot(lhs, rhs, lhs_dim, rhs_dim, precision=None):
    return lax.dot_general(
        lhs,
        rhs,
        (((lhs_dim,), (rhs_dim,)), ((), ())),
        precision=precision,
        preferred_element_type=f32,
    )


def loop(count, body):
    lax.fori_loop(0, count, lambda i, c: (body(i), c)[1], 0)


def kernel(
    h, tid, w, a, o, mag, cot,
    adapted, ig, gin, gout, gmag,
    wbuf, hbuf, obuf, lrs, lrr, lrb, sqs, sqr, sqb, sqf, slb, gbuf, cst, crecv,
    igacc, igs, igr, gpart, grecv, gx, gxr, gres, gms, gmr, gmx, gmxr,
    ring_send, ring_right, ring_left, h_send, h_recv, o_send, o_recv, lr_send, lr_recv,
    s1_send, s1_recv, s2_send, s2_recv, g_send, g_recv, f_send, c_send, c_recv,
    ig_send, ig_recv, rs_send, rs_recv, gx_send, gx_recv, ag_send, ag_recv,
    gm_send, gm_recv, gmx_send, gmx_recv,
    *, nt, nz,
):
    tok, ffl = h.shape
    adapt = a.shape[1]
    tenants = mag.shape[0]
    rank = adapt // tenants
    nm = nt // 2
    far = nz // 2
    half_rows = ffl // 2
    d = lax.axis_index("dp")
    t = lax.axis_index("tensor")
    yl = d // nz
    z = d % nz
    core = t % 2
    pair = (1 - yl) * nz + z
    mine = t % nm
    plane = t // nm
    in_plane = plane == yl

    def remote(src, dst, send, recv, dp, tensor):
        return pltpu.make_async_remote_copy(
            src_ref=src, dst_ref=dst, send_sem=send, recv_sem=recv,
            device_id=(dp, tensor), device_id_type=MESH,
        )

    def wait_in(ref, sem):
        pltpu.make_async_copy(ref, ref, sem).wait()

    wait_out = wait_in

    barrier = pltpu.get_barrier_semaphore()

    def greet_plane(i):
        s = i // nt
        u = i % nt

        @pl.when((s != yl) | (u != t))
        def _():
            pl.semaphore_signal(barrier, inc=1, device_id=(s * nz + z, u), device_id_type=MESH)

    def greet_column(i):
        @pl.when(i % nz != z)
        def _():
            pl.semaphore_signal(barrier, inc=1, device_id=(i, t), device_id_type=MESH)

    loop(2 * nt, greet_plane)
    loop(2 * nz, greet_column)
    pl.semaphore_wait(barrier, 2 * nt - 1 + 2 * (nz - 1))

    def ring(src, slot, half, step, right):
        rows = pl.ds(half * half_rows, half_rows)
        src = src.at[rows] if src is w else src.at[slot, rows]
        to = (z + (1 if right else nz - 1)) % nz
        sems = ring_right if right else ring_left
        return remote(
            src, wbuf.at[slot, rows], ring_send, sems.at[(step - 1) * 2 + half], yl * nz + to, t
        )

    def carried(step, half, right):
        return step < far or half == (0 if right else 1)

    def ring_step(step):
        for half in (0, 1):
            for right in (True, False):
                if not carried(step, half, right):
                    continue
                slot = (z + (nz - step if right else step)) % nz
                ring(wbuf, slot, half, step, right).wait_recv()
                if step < far and carried(step + 1, half, right):
                    ring(wbuf, slot, half, step + 1, right).start()

    for half in (0, 1):
        for right in (True, False):
            if carried(1, half, right):
                ring(w, z, half, 1, right).start()

    @pl.when(in_plane)
    def _():
        def send(u):
            @pl.when(u != t)
            def _():
                remote(o, obuf.at[mine], o_send, o_recv, d, u).start()

        loop(nt, send)
        obuf[mine] = o[...]

    remote(h, hbuf.at[yl], h_send, h_recv, pair, t).start()

    owner = lax.div(lax.broadcasted_iota(jnp.int32, (tok, adapt), 1), rank)
    row_owner = lax.div(lax.broadcasted_iota(jnp.int32, (adapt, tok), 0), rank)
    tenant = tid[d // 2]

    lr = jnp.where(owner == tenant, dot(h[...], a[...], 1, 0), 0.0)
    lrb[yl] = lr.astype(bf16)
    turned = lr.T
    packed = turned[0:rank]
    for k in range(1, tenants):
        packed = packed + turned[k * rank:(k + 1) * rank]
    lrs[...] = packed.astype(bf16)

    def send_lr(u):
        @pl.when(u != t)
        def _():
            remote(lrs, lrr.at[t], lr_send, lr_recv, d, u).start()

    loop(nt, send_lr)
    lrr[t] = lrs[...]
    wbuf[z] = w[...]
    hbuf[yl] = h[...]
    grow = lax.div(lax.broadcasted_iota(jnp.int32, (adapt, adapt), 0), rank)
    gcol = lax.div(lax.broadcasted_iota(jnp.int32, (adapt, adapt), 1), rank)
    gram = jnp.where(grow == gcol, dot(a[...], a[...], 0, 0), 0.0)
    cross = dot(a[...], w[...], 0, 0)
    wide = w[...].astype(f32)
    column_sq = jnp.sum(wide * wide, axis=0, keepdims=True)

    ring_step(1)

    @pl.when(in_plane)
    def _():
        wait_in(obuf.at[pl.ds(0, nm - 1)], o_recv)

    @pl.when(jnp.logical_not(in_plane))
    def _():
        wait_in(obuf.at[pl.ds(0, nm)], o_recv)

    own = obuf[z // 2, :, pl.ds(pl.multiple_of((z % 2) * 128, 128), 128)].astype(f32)
    inner = dot(gram, own, 1, 0, lax.Precision.HIGHEST)
    prod = (2.0 * cross + inner) * own
    rows = [
        jnp.sum(prod[k * rank:(k + 1) * rank], axis=0, keepdims=True) + column_sq
        for k in range(tenants)
    ]
    sqs[...] = jnp.concatenate(rows + [jnp.zeros((8 - tenants, 128), f32)], axis=0)
    lead = d // 2

    @pl.when(t != lead)
    def _():
        remote(sqs, sqr.at[t], s1_send, s1_recv, d, lead).start()

    @pl.when(t == lead)
    def _():
        sqr[t] = sqs[...]

    if far > 2:
        ring_step(2)

    @pl.when(t == lead)
    def _():
        wait_in(sqr.at[pl.ds(0, nt - 1)], s1_recv)
        total = sqr[0]
        for u in range(1, nt):
            total = total + sqr[u]
        sqb[...] = total

        def send(i):
            @pl.when(i != d)
            def _():
                remote(sqb, sqf.at[d % 2], s2_send, s2_recv.at[d % 2], i, t).start()

        loop(2 * nz, send)
        sqf[d % 2] = total

    if far > 3:
        ring_step(3)

    for e in (0, 1):
        @pl.when(d != 2 * t + e)
        def _(e=e):
            wait_in(sqf.at[e], s2_recv.at[e])

    squares = jnp.concatenate([sqf[0], sqf[1]], axis=1)[0:tenants]
    length = jnp.sqrt(squares + epsilon)
    col_scale = mag[...] / length
    one_hot = lax.broadcasted_iota(jnp.int32, (tenants, 256), 0) == tenant
    scale = jnp.sum(jnp.where(one_hot, col_scale, 0.0), axis=0, keepdims=True)
    slb[...] = (cot[...].astype(f32) * scale).astype(bf16)
    slot = mine * 2 + yl

    def send_slopes(q):
        u = 2 * q + core

        @pl.when(jnp.logical_not(in_plane) | (u != t))
        def _():
            remote(slb, gbuf.at[slot], g_send, g_recv.at[slot], plane * nz + z, u).start()

    loop(nt // 2, send_slopes)

    @pl.when(in_plane)
    def _():
        gbuf[slot] = slb[...]

    if far > 4:
        ring_step(4)

    wait_in(hbuf.at[1 - yl], h_recv)
    other = dot(hbuf[1 - yl], a[...], 1, 0)
    lrb[1 - yl] = jnp.where(owner == tid[pair // 2], other, 0.0).astype(bf16)

    def share(b):
        m = b // 2
        cols = pl.ds(pl.multiple_of((b % 2) * 128, 128), 128)
        for s in (0, 1):
            part = dot(hbuf[s], wbuf[b], 1, 0) + dot(lrb[s], obuf[m, :, cols], 1, 0)
            cst[b * 2 + s] = part.astype(bf16)
            here = (s == yl) & in_plane & (m == mine)

            @pl.when(here)
            def _():
                crecv[t * 2 + b % 2] = cst[b * 2 + s]

            @pl.when(jnp.logical_not(here))
            def _():
                remote(
                    cst.at[b * 2 + s], crecv.at[t * 2 + b % 2], c_send, c_recv,
                    s * nz + z, yl * nm + m,
                ).start()

    ready = min(4, far - 1)
    loop(2 * ready + 1, lambda i: share((z + nz - ready + i) % nz))

    def relay(i):
        at = (2 * (i // 2) + core) * 2 + i % 2

        @pl.when(jnp.logical_not(in_plane) | (at != slot))
        def _():
            wait_in(gbuf.at[at], g_recv.at[at])

        remote(gbuf.at[at], gbuf.at[at], f_send, g_recv.at[at], d, t + 1 - 2 * core).start()

    for step in range(ready + 1, far):
        ring_step(step)
        loop(2, lambda i: share((z + step + i * (2 * nz - 2 * step)) % nz))
    loop(nm, relay)

    def received(i):
        at = (2 * (i // 2) + 1 - core) * 2 + i % 2
        wait_in(gbuf.at[at], g_recv.at[at])

    loop(nm, received)

    def slopes_of(m):
        return jnp.concatenate([gbuf[2 * m], gbuf[2 * m + 1]], axis=0)

    back = dot(slopes_of(0), obuf[0], 1, 1)
    for m in range(1, nm):
        back = back + dot(slopes_of(m), obuf[m], 1, 1)
    tenant_col = jnp.concatenate(
        [jnp.full((tok, adapt), tid[(s * nz + z) // 2], jnp.int32) for s in (0, 1)], axis=0
    )
    owner2 = lax.div(lax.broadcasted_iota(jnp.int32, (2 * tok, adapt), 1), rank)
    back = jnp.where(owner2 == tenant_col, back, 0.0).astype(bf16)

    hidden2 = jnp.concatenate([hbuf[0], hbuf[1]], axis=0)
    grad_in = dot(hidden2, back, 0, 0)
    wait_in(lrr.at[pl.ds(0, nt - 1)], lr_recv)
    low = lrr[0].astype(f32)
    for u in range(1, nt):
        low = low + lrr[u].astype(f32)
    low = jnp.where(row_owner == tenant, jnp.concatenate([low] * tenants, axis=0), 0.0)
    high = low.astype(bf16)
    rest = (low - high.astype(f32)).astype(bf16)
    grad_out = dot(high, slb[...], 1, 0) + dot(rest, slb[...], 1, 0)
    grad_out = jnp.concatenate([grad_out[:, 0:128], grad_out[:, 128:256]], axis=0)
    in_rows = ffl // nz
    out_rows = 2 * adapt // nz
    pad = gpart.shape[1] - in_rows - out_rows
    for i in range(nz):
        parts = [
            grad_out[i * out_rows:(i + 1) * out_rows],
            grad_in[i * in_rows:(i + 1) * in_rows],
        ]
        if pad:
            parts.append(jnp.zeros((pad, 128), f32))
        gpart[i] = jnp.concatenate(parts, axis=0).astype(bf16)
    grecv[z] = gpart[z]

    def scatter(i):
        @pl.when(i != z)
        def _():
            remote(gpart.at[i], grecv.at[z], rs_send, rs_recv, yl * nz + i, t).start()

    loop(nz, scatter)

    last = ((z + far) % nz) // 2

    def backward(m):
        weight = jnp.concatenate([wbuf[2 * m], wbuf[2 * m + 1]], axis=1)
        for s in (0, 1):
            igacc[s] += dot(gbuf[2 * m + s], weight, 1, 1)

    for s in (0, 1):
        igacc[s] = dot(back[s * tok:(s + 1) * tok], a[...], 1, 1)
    loop(nm - 1, lambda i: backward((last + 1 + i) % nm))

    ring_step(far)
    share((z + far) % nz)
    backward(last)
    igs[...] = igacc[1 - yl].astype(bf16)
    remote(igs, igr, ig_send, ig_recv, pair, t).start()

    @pl.when(in_plane)
    def _():
        wait_in(crecv.at[pl.ds(0, 2 * nt - 2)], c_recv)

    @pl.when(jnp.logical_not(in_plane))
    def _():
        wait_in(crecv, c_recv)

    sums = []
    for half in (0, 1):
        cols = slice(half * 128, (half + 1) * 128)
        total = crecv[half].astype(f32)
        for u in range(1, nt):
            total = total + crecv[2 * u + half].astype(f32)
        adapted[:, cols] = (total * scale[:, cols]).astype(bf16)
        sums.append(jnp.sum(cot[:, cols].astype(f32) * total, axis=0, keepdims=True))
    hot = lax.broadcasted_iota(jnp.int32, (tenants, 128), 0) == tenant
    gms[...] = jnp.concatenate([jnp.where(hot, part, 0.0) for part in sums], axis=0)
    gmr[z] = gms[...]

    def send_mag(i):
        @pl.when(i != z)
        def _():
            remote(gms, gmr.at[z], gm_send, gm_recv, yl * nz + i, t).start()

    loop(nz, send_mag)

    wait_in(grecv.at[pl.ds(0, nz - 1)], rs_recv)
    total = grecv[0].astype(f32)
    for i in range(1, nz):
        total = total + grecv[i].astype(f32)
    gx[...] = total
    remote(gx, gxr, gx_send, gx_recv, pair, t).start()

    wait_in(igr, ig_recv)
    ig[...] = (igacc[yl] + igr[...].astype(f32)).astype(bf16)

    wait_in(gxr, gx_recv)
    gres[z] = (gx[...] + gxr[...]).astype(bf16)

    def spread(i):
        @pl.when(i != z)
        def _():
            remote(gres.at[z], gres.at[z], ag_send, ag_recv, yl * nz + i, t).start()

    loop(nz, spread)

    wait_in(gmr.at[pl.ds(0, nz - 1)], gm_recv)
    total = gmr[0]
    for i in range(1, nz):
        total = total + gmr[i]
    gmx[...] = total
    remote(gmx, gmxr, gmx_send, gmx_recv, pair, t).start()
    wait_in(gmxr, gmx_recv)
    total = gmx[...] + gmxr[...]
    gmag[...] = jnp.concatenate([total[0:tenants], total[tenants:]], axis=1) / length

    wait_in(gres.at[pl.ds(0, nz - 1)], ag_recv)
    for i in range(nz):
        part = gres[i].astype(f32)
        half, row = divmod(i * out_rows, adapt)
        gout[row:row + out_rows, half * 128:(half + 1) * 128] = part[0:out_rows]
        gin[i * in_rows:(i + 1) * in_rows] = part[out_rows:out_rows + in_rows]

    wait_out(wbuf.at[pl.ds(0, nz - 1)], ring_send)
    wait_out(hbuf.at[0], h_send)

    @pl.when(in_plane)
    def _():
        wait_out(obuf.at[pl.ds(0, nt - 1)], o_send)
        wait_out(gbuf.at[pl.ds(0, nt // 2 - 1)], g_send)
        wait_out(cst.at[pl.ds(0, 2 * nz - 2)], c_send)

    @pl.when(jnp.logical_not(in_plane))
    def _():
        wait_out(gbuf.at[pl.ds(0, nt // 2)], g_send)
        wait_out(cst, c_send)

    wait_out(lrr.at[pl.ds(0, nt - 1)], lr_send)

    @pl.when(t != lead)
    def _():
        wait_out(sqs, s1_send)

    @pl.when(t == lead)
    def _():
        wait_out(sqr.at[pl.ds(0, 2 * nz - 1)], s2_send)

    wait_out(gbuf.at[pl.ds(0, nm)], f_send)
    wait_out(igs, ig_send)
    wait_out(gpart.at[pl.ds(0, nz - 1)], rs_send)
    wait_out(gx, gx_send)
    wait_out(gres.at[pl.ds(0, nz - 1)], ag_send)
    wait_out(gmr.at[pl.ds(0, nz - 1)], gm_send)
    wait_out(gmx, gmx_send)


def per_device(nt, nz, hidden, tenant_ids, base_weight, adapter_in, adapter_out, magnitude, cotangent):
    tok, ffl = hidden.shape
    adapt = adapter_in.shape[1]
    nm = nt // 2
    grad_rows = -(-(ffl // nz + 2 * adapt // nz) // 16) * 16
    vmem = pl.BlockSpec(memory_space=pltpu.VMEM)
    dma = pltpu.SemaphoreType.DMA
    tile = (8, 128)
    scratch = [
        pltpu.VMEM((nz, ffl, 128), bf16),
        pltpu.VMEM((2, tok, ffl), bf16),
        pltpu.VMEM((nt, adapt, 256), bf16),
        pltpu.VMEM((adapt // 4, tok), bf16),
        pltpu.VMEM((nt, adapt // 4, tok), bf16),
        pltpu.VMEM((2, tok, adapt), bf16),
        pltpu.VMEM(tile, f32),
        pltpu.VMEM((2 * nz,) + tile, f32),
        pltpu.VMEM(tile, f32),
        pltpu.VMEM((2,) + tile, f32),
        pltpu.VMEM((tok, 256), bf16),
        pltpu.VMEM((nt, tok, 256), bf16),
        pltpu.VMEM((2 * nz, tok, 128), bf16),
        pltpu.VMEM((2 * nt, tok, 128), bf16),
        pltpu.VMEM((2, tok, ffl), f32),
        pltpu.VMEM((tok, ffl), bf16),
        pltpu.VMEM((tok, ffl), bf16),
        pltpu.VMEM((nz, grad_rows, 128), bf16),
        pltpu.VMEM((nz, grad_rows, 128), bf16),
        pltpu.VMEM((grad_rows, 128), f32),
        pltpu.VMEM((grad_rows, 128), f32),
        pltpu.VMEM((nz, grad_rows, 128), bf16),
        pltpu.VMEM(tile, f32),
        pltpu.VMEM((nz,) + tile, f32),
        pltpu.VMEM(tile, f32),
        pltpu.VMEM(tile, f32),
        dma, dma((nz,)), dma((nz,)), dma, dma, dma, dma, dma, dma,
        dma, dma, dma, dma((2,)), dma, dma((nt,)), dma, dma, dma,
        dma, dma, dma, dma, dma, dma, dma, dma,
        dma, dma, dma, dma,
    ]
    return pl.pallas_call(
        functools.partial(kernel, nt=nt, nz=nz),
        out_shape=(
            jax.ShapeDtypeStruct((tok, 256), bf16),
            jax.ShapeDtypeStruct((tok, ffl), bf16),
            jax.ShapeDtypeStruct((ffl, adapt), f32),
            jax.ShapeDtypeStruct((adapt, 256), f32),
            jax.ShapeDtypeStruct(magnitude.shape, f32),
        ),
        in_specs=[vmem, pl.BlockSpec(memory_space=pltpu.SMEM)] + [vmem] * 5,
        out_specs=[vmem] * 5,
        scratch_shapes=scratch,
        compiler_params=pltpu.CompilerParams(
            collective_id=0, has_side_effects=True, vmem_limit_bytes=48 * 2**20
        ),
        name="dora",
    )(hidden, tenant_ids, base_weight, adapter_in, adapter_out, magnitude, cotangent)


def solution(mesh):
    nt = mesh.shape["tensor"]
    nz = mesh.shape["dp"] // 2
    return jax.shard_map(
        functools.partial(per_device, nt, nz),
        mesh=mesh,
        in_specs=(
            P("dp", "tensor"),
            P(),
            P("tensor", "dp"),
            P("tensor", None),
            P(None, "tensor"),
            P(None, "tensor"),
            P("dp", "tensor"),
        ),
        out_specs=(
            P("dp", "tensor"),
            P("dp", "tensor"),
            P("tensor", None),
            P(None, "tensor"),
            P(None, "tensor"),
        ),
        check_vma=False,
    )
```

time: 834 us -> 138 us (0.17)
  the two profiles are of different devices: /device:TPU:2 before, /device:TPU:132 now
where the time goes in v1:
time: 138 us; the launch traced here: 137 us
  Pallas kernels  127 us (92%)
  local copies, waits for them, and re-layouts  9.41 us (7%)
    pallas_call x1, Pallas kernels, per_device(): pl.pallas_call(functools.partial(kernel, nt=nt, nz=nz), out_shape=(jax.Sh...  127 us
    unnamed x19, local copies, waits for them, and re-layouts  9.41 us

profile of v1, /device:TPU:132, one launch (start us, length us, event | category | flops | bytes accessed | tf_op | source)
XLA Modules:
  0.0 137.2 jit_solution(9667161413053800056)
XLA Ops:
  0.6 0.0 copy-start
  0.6 1.0 copy-done
  1.7 0.0 copy-start.1
  1.7 0.9 copy-done.1
  2.6 0.0 copy-start.2
  2.6 0.9 copy-done.2
  3.5 0.0 copy-start.3
  3.5 0.9 copy-done.3
  4.4 0.0 copy-start.4
  4.4 0.8 copy-done.4
  5.3 0.0 copy-start.5
  5.3 0.7 copy-done.5
  6.0 0.0 copy-start.6
  6.0 0.7 copy-done.6
  6.6 127.2 %dora.1 = (bf16[256,256]{1,0:T(8,128)(2,1)S(1)}, bf16[256,896]{1,0:T(8,128)(2,1)S(1)}, f32[896,128]{1,0:T(8,128)S(1)}, f32[128,256]{1,0:T(8,128)S(1)}, f32[4,256]{1,0:T(4,128)S(1)}) custom-call(bf16[256,896]{1,0:T(8,128)(2,1)S(1)} %copy-done, s32[16]{0:T(128)S(1)} %copy-done.6, bf16[896,128]{1,0:T(8,128)(2,1)S(1)} %copy-done.1, ...), custom_call_target="tpu_custom_call" | custom-call | tf_op jit(solution)/shard_map/dora/pallas_call | solution.py:477
  133.8 0.7 copy.17
  134.5 0.8 copy.18
  135.2 0.8 copy.19
  136.0 0.7 copy.20
  136.6 0.6 copy.21
Async XLA Ops:
  0.6 1.0 copy-start
  1.7 0.9 copy-start.1
  2.6 0.9 copy-start.2
  3.5 0.9 copy-start.3
  4.4 0.8 copy-start.4
  5.3 0.7 copy-start.5
  6.0 0.7 copy-start.6

commit v2 on v1

v2 whole, which is shorter than its diff:
```python
import functools

import jax
import jax.numpy as jnp
from jax import lax
from jax.experimental import pallas as pl
from jax.experimental.pallas import tpu as pltpu
from jax.sharding import PartitionSpec as P

epsilon = 1e-06
f32 = jnp.float32
bf16 = jnp.bfloat16
MESH = pl.DeviceIdType.MESH


def dot(lhs, rhs, lhs_dim, rhs_dim, precision=None):
    return lax.dot_general(
        lhs,
        rhs,
        (((lhs_dim,), (rhs_dim,)), ((), ())),
        precision=precision,
        preferred_element_type=f32,
    )


def loop(count, body):
    lax.fori_loop(0, count, lambda i, c: (body(i), c)[1], 0)


def kernel(
    h_hbm, tid, w_hbm, a_hbm, o_hbm, mag_hbm, cot_hbm,
    adapted, ig, gin, gout, gmag,
    a, o, mag, cot, wbuf, hbuf, ob, obd, lrs, lrr, bas, bar, sqs, sqr, sqb, sqf, slb, gbuf,
    cacc, sst, srecv, cst, crecv, igacc, igs, igr, gpart, grecv, gx, gxr, gres, gt,
    gms, gmr, gmx, gmxr,
    in_sem, ring_send, ring_right, ring_left, h_send, h_recv, o_send, o_recv,
    lr_send, lr_recv, ba_send, ba_recv, s1_send, s1_recv, s2_send, s2_recv,
    g_send, g_recv, f_send, sib_send, sib_recv, c_send, c_recv, ig_send, ig_recv,
    rs_send, rs_recv, gx_send, gx_recv, ag_send, ag_recv, gm_send, gm_recv, gmx_send, gmx_recv,
    *, nt, nz,
):
    tok, ffl = igs.shape
    adapt = a.shape[1]
    tenants = mag.shape[0]
    rank = adapt // tenants
    nm = nt // 2
    far = nz // 2
    half_rows = ffl // 2
    d = lax.axis_index("dp")
    t = lax.axis_index("tensor")
    yl = d // nz
    z = d % nz
    core = t % 2
    pair = (1 - yl) * nz + z
    sibling = t + 1 - 2 * core
    mine = t % nm
    plane = t // nm
    in_plane = plane == yl

    def remote(src, dst, send, recv, dp, tensor):
        return pltpu.make_async_remote_copy(
            src_ref=src, dst_ref=dst, send_sem=send, recv_sem=recv,
            device_id=(dp, tensor), device_id_type=MESH,
        )

    def wait_in(ref, sem):
        pltpu.make_async_copy(ref, ref, sem).wait()

    wait_out = wait_in

    loads = [
        pltpu.make_async_copy(src, dst, in_sem.at[i])
        for i, (src, dst) in enumerate((
            (w_hbm, wbuf.at[z]), (h_hbm, hbuf.at[yl]), (a_hbm, a), (o_hbm, o),
            (mag_hbm, mag), (cot_hbm, cot),
        ))
    ]
    for load in loads:
        load.start()

    barrier = pltpu.get_barrier_semaphore()

    def greet_plane(i):
        s = i // nt
        u = i % nt

        @pl.when((s != yl) | (u != t))
        def _():
            pl.semaphore_signal(barrier, inc=1, device_id=(s * nz + z, u), device_id_type=MESH)

    def greet_column(i):
        @pl.when(i % nz != z)
        def _():
            pl.semaphore_signal(barrier, inc=1, device_id=(i, t), device_id_type=MESH)

    loop(2 * nt, greet_plane)
    loop(2 * nz, greet_column)
    for load in loads:
        load.wait()
    pl.semaphore_wait(barrier, 2 * nt - 1 + 2 * (nz - 1))

    def ring(slot, half, step, right):
        rows = pl.ds(half * half_rows, half_rows)
        to = (z + (1 if right else nz - 1)) % nz
        sems = ring_right if right else ring_left
        ref = wbuf.at[slot, rows]
        return remote(ref, ref, ring_send, sems.at[(step - 1) * 2 + half], yl * nz + to, t)

    def carried(step, half, right):
        return step < far or half == (0 if right else 1)

    def ring_step(step):
        for half in (0, 1):
            for right in (True, False):
                if not carried(step, half, right):
                    continue
                slot = (z + (nz - step if right else step)) % nz
                ring(slot, half, step, right).wait_recv()
                if step < far and carried(step + 1, half, right):
                    ring(slot, half, step + 1, right).start()

    for half in (0, 1):
        for right in (True, False):
            if carried(1, half, right):
                ring(z, half, 1, right).start()

    lead = d // 2
    ocols = pl.ds(pl.multiple_of((z % 2) * 128, 128), 128)

    @pl.when(t == lead)
    def _():
        ob[...] = o[:, ocols]

        def send(u):
            @pl.when(u != t)
            def _():
                remote(ob, ob, o_send, o_recv, d, u).start()

        loop(nt, send)

    remote(hbuf.at[yl], hbuf.at[yl], h_send, h_recv, pair, t).start()

    tenant = tid[d // 2]

    owner = lax.div(lax.broadcasted_iota(jnp.int32, (tok, adapt), 1), rank)
    turned = jnp.where(owner == tenant, dot(hbuf[yl], a[...], 1, 0), 0.0).T
    packed = turned[0:rank]
    for k in range(1, tenants):
        packed = packed + turned[k * rank:(k + 1) * rank]
    lrs[...] = packed.astype(bf16)

    def send_lr(u):
        @pl.when(u != t)
        def _():
            remote(lrs, lrr.at[t], lr_send, lr_recv, d, u).start()

    loop(nt, send_lr)
    lrr[t] = lrs[...]
    grow = lax.div(lax.broadcasted_iota(jnp.int32, (adapt, adapt), 0), rank)
    gcol = lax.div(lax.broadcasted_iota(jnp.int32, (adapt, adapt), 1), rank)
    gram = jnp.where(grow == gcol, dot(a[...], a[...], 0, 0), 0.0)
    cross = dot(a[...], wbuf[z], 0, 0)
    wide = wbuf[z].astype(f32)
    column_sq = jnp.sum(wide * wide, axis=0, keepdims=True)

    ring_step(1)

    @pl.when(t != lead)
    def _():
        wait_in(ob, o_recv)

    own = ob[...].astype(f32)
    inner = dot(gram, own, 1, 0, lax.Precision.HIGHEST)
    prod = (2.0 * cross + inner) * own
    rows = [
        jnp.sum(prod[k * rank:(k + 1) * rank], axis=0, keepdims=True) + column_sq
        for k in range(tenants)
    ]
    sqs[...] = jnp.concatenate(rows + [jnp.zeros((8 - tenants, 128), f32)], axis=0)

    @pl.when(t != lead)
    def _():
        remote(sqs, sqr.at[t], s1_send, s1_recv, d, lead).start()

    @pl.when(t == lead)
    def _():
        sqr[t] = sqs[...]

    if far > 2:
        ring_step(2)

    @pl.when(t == lead)
    def _():
        wait_in(sqr.at[pl.ds(0, nt - 1)], s1_recv)
        total = sqr[0]
        for u in range(1, nt):
            total = total + sqr[u]
        sqb[...] = total

        def send(i):
            to = (i % 2) * nz + (z + far + (i // 4) * (1 - (i // 2) % 2 * 2) + nz - (i // 2) % 2) % nz

            @pl.when(to != d)
            def _():
                remote(sqb, sqf.at[d % 2], s2_send, s2_recv.at[d % 2], to, t).start()

        loop(2 * nz, send)
        sqf[d % 2] = total

    def share(b):
        sst[b] = dot(hbuf[1 - core], wbuf[b], 1, 0).astype(bf16)
        remote(sst.at[b], srecv.at[b], sib_send, sib_recv.at[b], d, sibling).start()
        cacc[b] = dot(hbuf[core], wbuf[b], 1, 0)

    def deliver(b):
        m = b // 2
        place = (t // 2) * 2 + b % 2
        wait_in(srecv.at[b], sib_recv.at[b])
        cst[b] = (cacc[b] + srecv[b].astype(f32)).astype(bf16)
        here = (core == yl) & in_plane & (m == mine)

        @pl.when(here)
        def _():
            crecv[place] = cst[b]

        @pl.when(jnp.logical_not(here))
        def _():
            remote(
                cst.at[b], crecv.at[place], c_send, c_recv, core * nz + z, yl * nm + m
            ).start()

    def near(step):
        return 2 * step + 1, lambda i: (z + nz - step + i) % nz

    def at(step):
        return 2, lambda i: (z + step + i * (2 * nz - 2 * step)) % nz

    def each(blocks, body):
        loop(blocks[0], lambda i: body(blocks[1](i)))

    ready = min(3, far - 1)
    if far > 3:
        ring_step(3)
    wait_in(hbuf.at[1 - yl], h_recv)
    each(near(ready), share)
    if far > 4:
        ring_step(4)

    for e in (0, 1):
        @pl.when(d != 2 * t + e)
        def _(e=e):
            wait_in(sqf.at[e], s2_recv.at[e])

    squares = jnp.concatenate([sqf[0], sqf[1]], axis=1)[0:tenants]
    length = jnp.sqrt(squares + epsilon)
    col_scale = mag[...] / length
    one_hot = lax.broadcasted_iota(jnp.int32, (tenants, 256), 0) == tenant
    scale = jnp.sum(jnp.where(one_hot, col_scale, 0.0), axis=0, keepdims=True)
    slb[...] = (cot[...].astype(f32) * scale).astype(bf16)
    slot = mine * 2 + yl

    def send_slopes(q):
        u = 2 * q + core

        @pl.when(jnp.logical_not(in_plane) | (u != t))
        def _():
            remote(slb, gbuf.at[slot], g_send, g_recv.at[slot], plane * nz + z, u).start()

    loop(nt // 2, send_slopes)

    @pl.when(in_plane)
    def _():
        gbuf[slot] = slb[...]

    out_ten = jnp.zeros((rank, 256), f32)
    for k in range(tenants):
        out_ten = jnp.where(tenant == k, o[k * rank:(k + 1) * rank].astype(f32), out_ten)
    out_ten = out_ten.astype(bf16)
    bas[...] = dot(out_ten, slb[...], 1, 1).astype(bf16)

    def send_back(u):
        @pl.when(u != t)
        def _():
            remote(bas, bar.at[t], ba_send, ba_recv, d, u).start()

    loop(nt, send_back)
    bar[t] = bas[...]

    if far > 5:
        ring_step(5)
    each(near(ready), deliver)
    for step in range(ready + 1, min(far, 6)):
        each(at(step), share)
    if far > 6:
        ring_step(6)
        for step in range(ready + 1, 6):
            each(at(step), deliver)
        each(at(6), share)

    wait_in(bar.at[pl.ds(0, nt - 1)], ba_recv)
    back = bar[0].astype(f32)
    for u in range(1, nt):
        back = back + bar[u].astype(f32)
    wait_in(lrr.at[pl.ds(0, nt - 1)], lr_recv)
    low = lrr[0].astype(f32)
    for u in range(1, nt):
        low = low + lrr[u].astype(f32)
    low_high = low.astype(bf16)
    low_rest = (low - low_high.astype(f32)).astype(bf16)
    back_high = back.astype(bf16)
    back_rest = (back - back_high.astype(f32)).astype(bf16)
    grads = [
        dot(back_high, hbuf[yl], 1, 0) + dot(back_rest, hbuf[yl], 1, 0),
        dot(low_high, slb[...], 1, 0) + dot(low_rest, slb[...], 1, 0),
    ]
    tiles = []
    for grad in grads:
        for j in range(grad.shape[1] // 128):
            for g in range(rank // 8):
                tiles.append(grad[g * 8:(g + 1) * 8, j * 128:(j + 1) * 128])
    per = gx.shape[0] // (8 * tenants)
    owners = len(tiles) // per
    for i in range(owners):
        parts = tiles[i * per:(i + 1) * per]
        parts.append(jnp.zeros((gpart.shape[1] - 8 * per, 128), f32))
        gpart[i] = jnp.concatenate(parts, axis=0).astype(bf16)

    def scatter(i):
        @pl.when(i != z)
        def _():
            remote(gpart.at[i], grecv.at[z], rs_send, rs_recv, yl * nz + i, t).start()

    loop(owners, scatter)

    @pl.when(z < owners)
    def _():
        grecv[z] = gpart[z]

    if far > 7:
        ring_step(7)
        each(at(6), deliver)
        each(at(7), share)

    row_owner = lax.div(lax.broadcasted_iota(jnp.int32, (adapt, tok), 0), rank)
    full = jnp.where(row_owner == tenant, jnp.concatenate([back] * tenants, axis=0), 0.0)
    igacc[yl] = dot(full.T.astype(bf16), a[...], 1, 1)
    igacc[1 - yl] = jnp.zeros((tok, ffl), f32)
    low_out = dot(low_high, out_ten, 0, 0) + dot(low_rest, out_ten, 0, 0)
    if far > 7:
        each(at(7), deliver)

    ring_step(far)
    share((z + far) % nz)

    def relay(i):
        at = (2 * (i // 2) + core) * 2 + i % 2

        @pl.when(jnp.logical_not(in_plane) | (at != slot))
        def _():
            wait_in(gbuf.at[at], g_recv.at[at])

        remote(gbuf.at[at], gbuf.at[at], f_send, g_recv.at[at], d, sibling).start()

    def received(i):
        at = (2 * (i // 2) + 1 - core) * 2 + i % 2
        wait_in(gbuf.at[at], g_recv.at[at])

    loop(nm, relay)
    deliver((z + far) % nz)
    loop(nm, received)

    def backward(s):
        def body(m):
            weight = jnp.concatenate([wbuf[2 * m], wbuf[2 * m + 1]], axis=1)
            igacc[s] += dot(gbuf[2 * m + s], weight, 1, 1)

        return body

    loop(nm, backward(1 - yl))
    igs[...] = igacc[1 - yl].astype(bf16)
    remote(igs, igr, ig_send, ig_recv, pair, t).start()

    @pl.when(z < owners)
    def _():
        wait_in(grecv.at[pl.ds(0, nz - 1)], rs_recv)
        sums = [jnp.zeros((8 * per, 128), f32)] * tenants
        for i in range(0, nz, 2):
            both = grecv[i].astype(f32) + grecv[i + 1].astype(f32)
            who = tid[(yl * nz + i) // 2]
            sums = [acc + jnp.where(who == k, both[0:8 * per], 0.0) for k, acc in enumerate(sums)]
        gx[...] = jnp.concatenate(sums, axis=0)
        remote(gx, gxr, gx_send, gx_recv, pair, t).start()

    here = in_plane & (core == yl)

    @pl.when(here)
    def _():
        wait_in(crecv.at[pl.ds(0, nt - 2)], c_recv)

    @pl.when(jnp.logical_not(here))
    def _():
        wait_in(crecv, c_recv)

    sums = []
    for half in (0, 1):
        cols = slice(half * 128, (half + 1) * 128)
        total = low_out[:, cols]
        for q in range(nt // 2):
            total = total + crecv[2 * q + half].astype(f32)
        adapted[:, cols] = (total * scale[:, cols]).astype(bf16)
        sums.append(jnp.sum(cot[:, cols].astype(f32) * total, axis=0, keepdims=True))
    hot = lax.broadcasted_iota(jnp.int32, (tenants, 128), 0) == tenant
    gms[...] = jnp.concatenate([jnp.where(hot, part, 0.0) for part in sums], axis=0)

    def send_mag(i):
        to = (z + far + i) % nz

        @pl.when(to != z)
        def _():
            remote(gms, gmr.at[z], gm_send, gm_recv, yl * nz + to, t).start()

    loop(nz, send_mag)
    gmr[z] = gms[...]

    @pl.when(z < owners)
    def _():
        wait_in(gxr, gx_recv)
        gres[z] = (gx[...] + gxr[...]).astype(bf16)

        def spread(i):
            to = (z + far + i) % nz

            @pl.when(to != z)
            def _():
                remote(gres.at[z], gres.at[z], ag_send, ag_recv, yl * nz + to, t).start()

        loop(nz, spread)

    loop(nm, backward(yl))
    wait_in(gmr.at[pl.ds(0, nz - 1)], gm_recv)
    total = gmr[0]
    for i in range(1, nz):
        total = total + gmr[i]
    gmx[...] = total
    remote(gmx, gmxr, gmx_send, gmx_recv, pair, t).start()

    wait_in(igr, ig_recv)
    ig[...] = (igacc[yl] + igr[...].astype(f32)).astype(bf16)

    @pl.when(z < owners)
    def _():
        wait_in(gres.at[pl.ds(0, owners - 1)], ag_recv)

    @pl.when(z >= owners)
    def _():
        wait_in(gres.at[pl.ds(0, owners)], ag_recv)

    for i in range(len(tiles)):
        j, g = divmod(i, rank // 8)
        part = gres[i // per].astype(f32)
        for k in range(tenants):
            row = k * rank + g * 8
            src = (k * per + i % per) * 8
            if j < ffl // 128:
                gt[row:row + 8, j * 128:(j + 1) * 128] = part[src:src + 8]
            else:
                j2 = j - ffl // 128
                gout[row:row + 8, j2 * 128:(j2 + 1) * 128] = part[src:src + 8]
    for j in range(ffl // 128):
        gin[j * 128:(j + 1) * 128] = gt[:, j * 128:(j + 1) * 128].T

    wait_in(gmxr, gmx_recv)
    total = gmx[...] + gmxr[...]
    gmag[...] = jnp.concatenate([total[0:tenants], total[tenants:]], axis=1) / length

    wait_out(wbuf.at[pl.ds(0, nz - 1)], ring_send)
    wait_out(hbuf.at[0], h_send)

    @pl.when(t != lead)
    def _():
        wait_out(sqs, s1_send)

    @pl.when(t == lead)
    def _():
        wait_out(obd.at[pl.ds(0, nt - 1)], o_send)
        wait_out(sqr.at[pl.ds(0, 2 * nz - 1)], s2_send)

    wait_out(lrr.at[pl.ds(0, nt - 1)], lr_send)
    wait_out(bar.at[pl.ds(0, nt - 1)], ba_send)

    @pl.when(in_plane)
    def _():
        wait_out(gbuf.at[pl.ds(0, nt // 2 - 1)], g_send)

    @pl.when(jnp.logical_not(in_plane))
    def _():
        wait_out(gbuf.at[pl.ds(0, nt // 2)], g_send)

    wait_out(gbuf.at[pl.ds(0, nm)], f_send)
    wait_out(sst, sib_send)

    @pl.when(here)
    def _():
        wait_out(cst.at[pl.ds(0, nz - 2)], c_send)

    @pl.when(jnp.logical_not(here))
    def _():
        wait_out(cst, c_send)

    wait_out(igs, ig_send)

    @pl.when(z < owners)
    def _():
        wait_out(gpart.at[pl.ds(0, owners - 1)], rs_send)
        wait_out(gx, gx_send)
        wait_out(gres.at[pl.ds(0, nz - 1)], ag_send)

    @pl.when(z >= owners)
    def _():
        wait_out(gpart.at[pl.ds(0, owners)], rs_send)

    wait_out(gmr.at[pl.ds(0, nz - 1)], gm_send)
    wait_out(gmx, gmx_send)


def per_device(nt, nz, hidden, tenant_ids, base_weight, adapter_in, adapter_out, magnitude, cotangent):
    tok, ffl = hidden.shape
    adapt = adapter_in.shape[1]
    tenants = magnitude.shape[0]
    rank = adapt // tenants
    tiles = (ffl // 128 + 2) * (rank // 8)
    per = 3
    while tiles > per * nz:
        per += 1
    while tiles % per:
        per += 1
    part_rows = -(-8 * per // 16) * 16
    vmem = pl.BlockSpec(memory_space=pltpu.VMEM)
    hbm = pl.BlockSpec(memory_space=pl.ANY)
    dma = pltpu.SemaphoreType.DMA
    tile = (8, 128)
    scratch = [
        pltpu.VMEM((ffl, adapt), bf16),
        pltpu.VMEM((adapt, 256), bf16),
        pltpu.VMEM((tenants, 256), f32),
        pltpu.VMEM((tok, 256), bf16),
        pltpu.VMEM((nz, ffl, 128), bf16),
        pltpu.VMEM((2, tok, ffl), bf16),
        pltpu.VMEM((adapt, 128), bf16),
        pltpu.VMEM((nt, adapt, 128), bf16),
        pltpu.VMEM((rank, tok), bf16),
        pltpu.VMEM((nt, rank, tok), bf16),
        pltpu.VMEM((rank, tok), bf16),
        pltpu.VMEM((nt, rank, tok), bf16),
        pltpu.VMEM(tile, f32),
        pltpu.VMEM((2 * nz,) + tile, f32),
        pltpu.VMEM(tile, f32),
        pltpu.VMEM((2,) + tile, f32),
        pltpu.VMEM((tok, 256), bf16),
        pltpu.VMEM((nt, tok, 256), bf16),
        pltpu.VMEM((nz, tok, 128), f32),
        pltpu.VMEM((nz, tok, 128), bf16),
        pltpu.VMEM((nz, tok, 128), bf16),
        pltpu.VMEM((nz, tok, 128), bf16),
        pltpu.VMEM((nt, tok, 128), bf16),
        pltpu.VMEM((2, tok, ffl), f32),
        pltpu.VMEM((tok, ffl), bf16),
        pltpu.VMEM((tok, ffl), bf16),
        pltpu.VMEM((nz, part_rows, 128), bf16),
        pltpu.VMEM((nz, part_rows, 128), bf16),
        pltpu.VMEM((tenants * per * 8, 128), f32),
        pltpu.VMEM((tenants * per * 8, 128), f32),
        pltpu.VMEM((nz, tenants * per * 8, 128), bf16),
        pltpu.VMEM((adapt, ffl), f32),
        pltpu.VMEM(tile, f32),
        pltpu.VMEM((nz,) + tile, f32),
        pltpu.VMEM(tile, f32),
        pltpu.VMEM(tile, f32),
        dma((6,)), dma, dma((nz,)), dma((nz,)), dma, dma, dma, dma,
        dma, dma, dma, dma, dma, dma, dma, dma((2,)),
        dma, dma((nt,)), dma, dma, dma((nz,)), dma, dma, dma, dma,
        dma, dma, dma, dma, dma, dma, dma, dma, dma, dma,
    ]
    return pl.pallas_call(
        functools.partial(kernel, nt=nt, nz=nz),
        out_shape=(
            jax.ShapeDtypeStruct((tok, 256), bf16),
            jax.ShapeDtypeStruct((tok, ffl), bf16),
            jax.ShapeDtypeStruct((ffl, adapt), f32),
            jax.ShapeDtypeStruct((adapt, 256), f32),
            jax.ShapeDtypeStruct(magnitude.shape, f32),
        ),
        in_specs=[hbm, pl.BlockSpec(memory_space=pltpu.SMEM)] + [hbm] * 5,
        out_specs=[vmem] * 5,
        scratch_shapes=scratch,
        compiler_params=pltpu.CompilerParams(
            collective_id=0, has_side_effects=True, vmem_limit_bytes=48 * 2**20
        ),
        name="dora",
    )(hidden, tenant_ids, base_weight, adapter_in, adapter_out, magnitude, cotangent)


def solution(mesh):
    nt = mesh.shape["tensor"]
    nz = mesh.shape["dp"] // 2
    return jax.shard_map(
        functools.partial(per_device, nt, nz),
        mesh=mesh,
        in_specs=(
            P("dp", "tensor"),
            P(),
            P("tensor", "dp"),
            P("tensor", None),
            P(None, "tensor"),
            P(None, "tensor"),
            P("dp", "tensor"),
        ),
        out_specs=(
            P("dp", "tensor"),
            P("dp", "tensor"),
            P("tensor", None),
            P(None, "tensor"),
            P(None, "tensor"),
        ),
        check_vma=False,
    )
```

time: 138 us -> 133 us (0.964)
  the two profiles are of different devices: /device:TPU:132 before, /device:TPU:6 now
where the time goes in v2:
time: 133 us
  Pallas kernels  123 us (92%)
  local copies, waits for them, and re-layouts  9.41 us (7%)
    pallas_call x1, Pallas kernels, per_device(): pl.pallas_call(functools.partial(kernel, nt=nt, nz=nz), out_shape=(jax.Sh...  123 us
    unnamed x19, local copies, waits for them, and re-layouts  9.41 us

profile of v2, /device:TPU:6, one launch (start us, length us, event | category | flops | bytes accessed | tf_op | source)
XLA Modules:
  0.0 132.9 jit_solution(7553336917723155395)
XLA Ops:
  0.6 0.0 copy-start
  0.6 1.0 copy-done
  1.7 0.0 copy-start.1
  1.7 0.9 copy-done.1
  2.6 0.0 copy-start.2
  2.6 0.9 copy-done.2
  3.5 0.0 copy-start.3
  3.5 0.9 copy-done.3
  4.4 0.0 copy-start.4
  4.4 0.8 copy-done.4
  5.3 0.0 copy-start.5
  5.3 0.7 copy-done.5
  6.0 0.0 copy-start.6
  6.0 0.7 copy-done.6
  6.6 122.8 %dora.1 = (bf16[256,256]{1,0:T(8,128)(2,1)S(1)}, bf16[256,896]{1,0:T(8,128)(2,1)S(1)}, f32[896,128]{1,0:T(8,128)S(1)}, f32[128,256]{1,0:T(8,128)S(1)}, f32[4,256]{1,0:T(4,128)S(1)}) custom-call(bf16[256,896]{1,0:T(8,128)(2,1)S(1)} %copy-done, s32[16]{0:T(128)S(1)} %copy-done.6, bf16[896,128]{1,0:T(8,128)(2,1)S(1)} %copy-done.1, ...), custom_call_target="tpu_custom_call" | custom-call | tf_op jit(solution)/shard_map/dora/pallas_call | solution.py:584
  129.4 0.7 copy.17
  130.1 0.8 copy.18
  130.9 0.8 copy.19
  131.6 0.7 copy.20
  132.3 0.6 copy.21
Async XLA Ops:
  0.6 1.0 copy-start
  1.7 0.9 copy-start.1
  2.6 0.9 copy-start.2
  3.5 0.9 copy-start.3
  4.4 0.8 copy-start.4
  5.3 0.7 copy-start.5
  6.0 0.7 copy-start.6

commit v3 on v2

--- a/solution.py
+++ b/solution.py
@@ -31,7 +31,7 @@
     h_hbm, tid, w_hbm, a_hbm, o_hbm, mag_hbm, cot_hbm,
     adapted, ig, gin, gout, gmag,
     a, o, mag, cot, wbuf, hbuf, ob, obd, lrs, lrr, bas, bar, sqs, sqr, sqb, sqf, slb, gbuf,
-    cacc, sst, srecv, cst, crecv, igacc, igs, igr, gpart, grecv, gx, gxr, gres, gt,
+    cacc, sst, srecv, cst, crecv, igacc, igs, igr, gpart, grecv, gres, agd, gt,
     gms, gmr, gmx, gmxr,
     in_sem, ring_send, ring_right, ring_left, h_send, h_recv, o_send, o_recv,
     lr_send, lr_recv, ba_send, ba_recv, s1_send, s1_recv, s2_send, s2_recv,
@@ -138,8 +138,6 @@
 
         loop(nt, send)
 
-    remote(hbuf.at[yl], hbuf.at[yl], h_send, h_recv, pair, t).start()
-
     tenant = tid[d // 2]
 
     owner = lax.div(lax.broadcasted_iota(jnp.int32, (tok, adapt), 1), rank)
@@ -154,16 +152,12 @@
         def _():
             remote(lrs, lrr.at[t], lr_send, lr_recv, d, u).start()
 
-    loop(nt, send_lr)
-    lrr[t] = lrs[...]
     grow = lax.div(lax.broadcasted_iota(jnp.int32, (adapt, adapt), 0), rank)
     gcol = lax.div(lax.broadcasted_iota(jnp.int32, (adapt, adapt), 1), rank)
     gram = jnp.where(grow == gcol, dot(a[...], a[...], 0, 0), 0.0)
     cross = dot(a[...], wbuf[z], 0, 0)
     wide = wbuf[z].astype(f32)
     column_sq = jnp.sum(wide * wide, axis=0, keepdims=True)
-
-    ring_step(1)
 
     @pl.when(t != lead)
     def _():
@@ -186,8 +180,8 @@
     def _():
         sqr[t] = sqs[...]
 
-    if far > 2:
-        ring_step(2)
+    ring_step(1)
+    remote(hbuf.at[yl], hbuf.at[yl], h_send, h_recv, pair, t).start()
 
     @pl.when(t == lead)
     def _():
@@ -206,6 +200,11 @@
 
         loop(2 * nz, send)
         sqf[d % 2] = total
+
+    loop(nt, send_lr)
+    lrr[t] = lrs[...]
+    if far > 2:
+        ring_step(2)
 
     def share(b):
         sst[b] = dot(hbuf[1 - core], wbuf[b], 1, 0).astype(bf16)
@@ -241,10 +240,6 @@
     ready = min(3, far - 1)
     if far > 3:
         ring_step(3)
-    wait_in(hbuf.at[1 - yl], h_recv)
-    each(near(ready), share)
-    if far > 4:
-        ring_step(4)
 
     for e in (0, 1):
         @pl.when(d != 2 * t + e)
@@ -286,6 +281,10 @@
     loop(nt, send_back)
     bar[t] = bas[...]
 
+    if far > 4:
+        ring_step(4)
+    wait_in(hbuf.at[1 - yl], h_recv)
+    each(near(ready), share)
     if far > 5:
         ring_step(5)
     each(near(ready), deliver)
@@ -318,23 +317,25 @@
         for j in range(grad.shape[1] // 128):
             for g in range(rank // 8):
                 tiles.append(grad[g * 8:(g + 1) * 8, j * 128:(j + 1) * 128])
-    per = gx.shape[0] // (8 * tenants)
+    per = gpart.shape[1] // 8
     owners = len(tiles) // per
+    rank_of = 2 * z + yl
+    owns = rank_of < owners
     for i in range(owners):
-        parts = tiles[i * per:(i + 1) * per]
-        parts.append(jnp.zeros((gpart.shape[1] - 8 * per, 128), f32))
-        gpart[i] = jnp.concatenate(parts, axis=0).astype(bf16)
+        gpart[i] = jnp.concatenate(tiles[i * per:(i + 1) * per], axis=0).astype(bf16)
 
     def scatter(i):
-        @pl.when(i != z)
-        def _():
-            remote(gpart.at[i], grecv.at[z], rs_send, rs_recv, yl * nz + i, t).start()
+        to = (i % 2) * nz + i // 2
+
+        @pl.when(to != d)
+        def _():
+            remote(gpart.at[i], grecv.at[d], rs_send, rs_recv, to, t).start()
 
     loop(owners, scatter)
 
-    @pl.when(z < owners)
-    def _():
-        grecv[z] = gpart[z]
+    @pl.when(owns)
+    def _():
+        grecv[d] = gpart[rank_of]
 
     if far > 7:
         ring_step(7)
@@ -352,6 +353,30 @@
     ring_step(far)
     share((z + far) % nz)
 
+    held = owners // 2
+    ours = pl.ds(yl * held, held)
+    theirs = pl.ds((1 - yl) * held, held)
+
+    @pl.when(owns)
+    def _():
+        wait_in(grecv.at[pl.ds(0, 2 * nz - 1)], rs_recv)
+        sums = [jnp.zeros((8 * per, 128), f32)] * tenants
+        for i in range(nz):
+            both = grecv[2 * i].astype(f32) + grecv[2 * i + 1].astype(f32)
+            sums = [acc + jnp.where(tid[i] == k, both, 0.0) for k, acc in enumerate(sums)]
+        place = yl * held + z
+        gres[place] = jnp.concatenate(sums, axis=0).astype(bf16)
+
+        def spread(i):
+            to = (z + far + i) % nz
+
+            @pl.when(to != z)
+            def _():
+                remote(gres.at[place], gres.at[place], ag_send, ag_recv, yl * nz + to, t).start()
+
+        loop(nz, spread)
+
+
     def relay(i):
         at = (2 * (i // 2) + core) * 2 + i % 2
 
@@ -365,8 +390,9 @@
         at = (2 * (i // 2) + 1 - core) * 2 + i % 2
         wait_in(gbuf.at[at], g_recv.at[at])
 
+    deliver((z + far) % nz)
     loop(nm, relay)
-    deliver((z + far) % nz)
+
     loop(nm, received)
 
     def backward(s):
@@ -379,17 +405,6 @@
     loop(nm, backward(1 - yl))
     igs[...] = igacc[1 - yl].astype(bf16)
     remote(igs, igr, ig_send, ig_recv, pair, t).start()
-
-    @pl.when(z < owners)
-    def _():
-        wait_in(grecv.at[pl.ds(0, nz - 1)], rs_recv)
-        sums = [jnp.zeros((8 * per, 128), f32)] * tenants
-        for i in range(0, nz, 2):
-            both = grecv[i].astype(f32) + grecv[i + 1].astype(f32)
-            who = tid[(yl * nz + i) // 2]
-            sums = [acc + jnp.where(who == k, both[0:8 * per], 0.0) for k, acc in enumerate(sums)]
-        gx[...] = jnp.concatenate(sums, axis=0)
-        remote(gx, gxr, gx_send, gx_recv, pair, t).start()
 
     here = in_plane & (core == yl)
 
@@ -422,21 +437,17 @@
     loop(nz, send_mag)
     gmr[z] = gms[...]
 
-    @pl.when(z < owners)
-    def _():
-        wait_in(gxr, gx_recv)
-        gres[z] = (gx[...] + gxr[...]).astype(bf16)
-
-        def spread(i):
-            to = (z + far + i) % nz
-
-            @pl.when(to != z)
-            def _():
-                remote(gres.at[z], gres.at[z], ag_send, ag_recv, yl * nz + to, t).start()
-
-        loop(nz, spread)
-
     loop(nm, backward(yl))
+
+    @pl.when(owns)
+    def _():
+        wait_in(gres.at[pl.ds(0, held - 1)], ag_recv)
+
+    @pl.when(jnp.logical_not(owns))
+    def _():
+        wait_in(gres.at[ours], ag_recv)
+
+    remote(gres.at[ours], gres.at[ours], gx_send, gx_recv, pair, t).start()
     wait_in(gmr.at[pl.ds(0, nz - 1)], gm_recv)
     total = gmr[0]
     for i in range(1, nz):
@@ -447,17 +458,11 @@
     wait_in(igr, ig_recv)
     ig[...] = (igacc[yl] + igr[...].astype(f32)).astype(bf16)
 
-    @pl.when(z < owners)
-    def _():
-        wait_in(gres.at[pl.ds(0, owners - 1)], ag_recv)
-
-    @pl.when(z >= owners)
-    def _():
-        wait_in(gres.at[pl.ds(0, owners)], ag_recv)
-
+    wait_in(gres.at[theirs], gx_recv)
     for i in range(len(tiles)):
         j, g = divmod(i, rank // 8)
-        part = gres[i // per].astype(f32)
+        o_index = i // per
+        part = gres[o_index % 2 * held + o_index // 2].astype(f32)
         for k in range(tenants):
             row = k * rank + g * 8
             src = (k * per + i % per) * 8
@@ -509,16 +514,16 @@
 
     wait_out(igs, ig_send)
 
-    @pl.when(z < owners)
+    @pl.when(owns)
     def _():
         wait_out(gpart.at[pl.ds(0, owners - 1)], rs_send)
-        wait_out(gx, gx_send)
-        wait_out(gres.at[pl.ds(0, nz - 1)], ag_send)
-
-    @pl.when(z >= owners)
-    def _():
-        wait_out(gpart.at[pl.ds(0, owners)], rs_send)
-
+        wait_out(agd.at[pl.ds(0, nz - 1)], ag_send)
+
+    @pl.when(jnp.logical_not(owns))
+    def _():
+        wait_out(gpart, rs_send)
+
+    wait_out(gres.at[ours], gx_send)
     wait_out(gmr.at[pl.ds(0, nz - 1)], gm_send)
     wait_out(gmx, gmx_send)
 
@@ -529,12 +534,8 @@
     tenants = magnitude.shape[0]
     rank = adapt // tenants
     tiles = (ffl // 128 + 2) * (rank // 8)
-    per = 3
-    while tiles > per * nz:
-        per += 1
-    while tiles % per:
-        per += 1
-    part_rows = -(-8 * per // 16) * 16
+    per = 2
+    owners = tiles // per
     vmem = pl.BlockSpec(memory_space=pltpu.VMEM)
     hbm = pl.BlockSpec(memory_space=pl.ANY)
     dma = pltpu.SemaphoreType.DMA
@@ -566,10 +567,9 @@
         pltpu.VMEM((2, tok, ffl), f32),
         pltpu.VMEM((tok, ffl), bf16),
         pltpu.VMEM((tok, ffl), bf16),
-        pltpu.VMEM((nz, part_rows, 128), bf16),
-        pltpu.VMEM((nz, part_rows, 128), bf16),
-        pltpu.VMEM((tenants * per * 8, 128), f32),
-        pltpu.VMEM((tenants * per * 8, 128), f32),
+        pltpu.VMEM((owners, 8 * per, 128), bf16),
+        pltpu.VMEM((2 * nz, 8 * per, 128), bf16),
+        pltpu.VMEM((owners, tenants * per * 8, 128), bf16),
         pltpu.VMEM((nz, tenants * per * 8, 128), bf16),
         pltpu.VMEM((adapt, ffl), f32),
         pltpu.VMEM(tile, f32),

time: 133 us -> 112 us (0.84)
  the two profiles are of different devices: /device:TPU:6 before, /device:TPU:8 now
where the time goes in v3:
time: 112 us
  Pallas kernels  101 us (90%)
  local copies, waits for them, and re-layouts  9.41 us (8%)
    pallas_call x1, Pallas kernels, per_device(): pl.pallas_call(functools.partial(kernel, nt=nt, nz=nz), out_shape=(jax.Sh...  101 us
    unnamed x19, local copies, waits for them, and re-layouts  9.41 us

profile of v3, /device:TPU:8, one launch (start us, length us, event | category | flops | bytes accessed | tf_op | source)
XLA Modules:
  0.0 111.5 jit_solution(4097658775553717034)
XLA Ops:
  0.6 0.0 copy-start
  0.6 1.0 copy-done
  1.7 0.0 copy-start.1
  1.7 0.9 copy-done.1
  2.6 0.0 copy-start.2
  2.6 0.9 copy-done.2
  3.5 0.0 copy-start.3
  3.5 0.9 copy-done.3
  4.4 0.0 copy-start.4
  4.4 0.8 copy-done.4
  5.3 0.0 copy-start.5
  5.3 0.7 copy-done.5
  6.0 0.0 copy-start.6
  6.0 0.7 copy-done.6
  6.6 101.4 %dora.1 = (bf16[256,256]{1,0:T(8,128)(2,1)S(1)}, bf16[256,896]{1,0:T(8,128)(2,1)S(1)}, f32[896,128]{1,0:T(8,128)S(1)}, f32[128,256]{1,0:T(8,128)S(1)}, f32[4,256]{1,0:T(4,128)S(1)}) custom-call(bf16[256,896]{1,0:T(8,128)(2,1)S(1)} %copy-done, s32[16]{0:T(128)S(1)} %copy-done.6, bf16[896,128]{1,0:T(8,128)(2,1)S(1)} %copy-done.1, ...), custom_call_target="tpu_custom_call" | custom-call | tf_op jit(solution)/shard_map/dora/pallas_call | solution.py:584
  108.1 0.7 copy.17
  108.7 0.8 copy.18
  109.5 0.8 copy.19
  110.3 0.7 copy.20
  110.9 0.6 copy.21
Async XLA Ops:
  0.6 1.0 copy-start
  1.7 0.9 copy-start.1
  2.6 0.9 copy-start.2
  3.5 0.9 copy-start.3
  4.4 0.8 copy-start.4
  5.3 0.7 copy-start.5
  6.0 0.7 copy-start.6

commit v4 on v3

--- a/solution.py
+++ b/solution.py
@@ -526,6 +526,11 @@
     wait_out(gres.at[ours], gx_send)
     wait_out(gmr.at[pl.ds(0, nz - 1)], gm_send)
     wait_out(gmx, gmx_send)
+
+
+def hand_over(*refs):
+    for i in range(5):
+        refs[5 + i][...] = refs[i][...]
 
 
 def per_device(nt, nz, hidden, tenant_ids, base_weight, adapter_in, adapter_out, magnitude, cotangent):
@@ -581,7 +586,7 @@
         dma, dma((nt,)), dma, dma, dma((nz,)), dma, dma, dma, dma,
         dma, dma, dma, dma, dma, dma, dma, dma, dma, dma,
     ]
-    return pl.pallas_call(
+    results = pl.pallas_call(
         functools.partial(kernel, nt=nt, nz=nz),
         out_shape=(
             jax.ShapeDtypeStruct((tok, 256), bf16),
@@ -594,10 +599,18 @@
         out_specs=[vmem] * 5,
         scratch_shapes=scratch,
         compiler_params=pltpu.CompilerParams(
-            collective_id=0, has_side_effects=True, vmem_limit_bytes=48 * 2**20
+            collective_id=0, has_side_effects=True, vmem_limit_bytes=63 * 2**20
         ),
         name="dora",
     )(hidden, tenant_ids, base_weight, adapter_in, adapter_out, magnitude, cotangent)
+    return pl.pallas_call(
+        hand_over,
+        out_shape=[jax.ShapeDtypeStruct(r.shape, r.dtype) for r in results],
+        in_specs=[vmem] * 5,
+        out_specs=[vmem] * 5,
+        compiler_params=pltpu.CompilerParams(vmem_limit_bytes=63 * 2**20),
+        name="hand_over",
+    )(*results)
 
 
 def solution(mesh):

time: 112 us -> 106 us (0.946)
  local copies, waits for them, and re-layouts: 9.41 us -> 0 us
  Pallas kernels: 101 us -> 105 us
    unnamed x19 -> x0, local copies, waits for them, and re-layouts: 9.41 us -> none
    pallas_call x0 -> x1, Pallas kernels: none -> 2.31 us  [per_device(): pl.pallas_call(hand_over, out_shape=[jax.ShapeDtypeStruct(r.shape, r.dtyp...]
    pallas_call x1, Pallas kernels: 101 us -> 103 us  [per_device(): pl.pallas_call(functools.partial(kernel, nt=nt, nz=nz), out_shape=(jax.Sh...]
where the time goes in v4:
time: 106 us
  Pallas kernels  105 us (99%)
    pallas_call x1, Pallas kernels, per_device(): pl.pallas_call(functools.partial(kernel, nt=nt, nz=nz), out_shape=(jax.Sh...  103 us
    pallas_call x1, Pallas kernels, per_device(): pl.pallas_call(hand_over, out_shape=[jax.ShapeDtypeStruct(r.shape, r.dtyp...  2.31 us

profile of v4, /device:TPU:8, one launch (start us, length us, event | category | flops | bytes accessed | tf_op | source)
XLA Modules:
  0.0 105.5 jit_solution(12878387204001086824)
XLA Ops:
  0.6 102.6 %dora.1 = (bf16[256,256]{1,0:T(8,128)(2,1)}, bf16[256,896]{1,0:T(8,128)(2,1)}, f32[896,128]{1,0:T(8,128)}, f32[128,256]{1,0:T(8,128)}, f32[4,256]{1,0:T(4,128)}) custom-call(bf16[256,896]{1,0:T(8,128)(2,1)} %h_hbm.1, s32[16]{0:T(128)} %tid.1, bf16[896,128]{1,0:T(8,128)(2,1)} %w_hbm.1, bf16[896,128]{1,0:T(8,128)(2,1)} %a_hbm.1, bf16[128,256]{1,0:T(8,128)(2,1)} %o_hbm.1, ...), custom_call_target="tpu_custom_call" | custom-call | tf_op jit(solution)/shard_map/dora/pallas_call | solution.py:589
  103.2 2.3 %hand_over.1 = (bf16[256,256]{1,0:T(8,128)(2,1)}, bf16[256,896]{1,0:T(8,128)(2,1)}, f32[896,128]{1,0:T(8,128)}, f32[128,256]{1,0:T(8,128)}, f32[4,256]{1,0:T(4,128)}) custom-call(bf16[256,256]{1,0:T(8,128)(2,1)} %get-tuple-element.10.refs_0_, bf16[256,896]{1,0:T(8,128)(2,1)} %get-tuple-element.11.refs_1_, f32[896,128]{1,0:T(8,128)} %get-tuple-element.12.refs_2_, ...), custom_call_target="tpu_custom_call" | custom-call | tf_op jit(solution)/shard_map/hand_over/pallas_call | solution.py:606

commit v5 on v4

--- a/solution.py
+++ b/solution.py
@@ -238,8 +238,6 @@
         loop(blocks[0], lambda i: body(blocks[1](i)))
 
     ready = min(3, far - 1)
-    if far > 3:
-        ring_step(3)
 
     for e in (0, 1):
         @pl.when(d != 2 * t + e)
@@ -281,6 +279,8 @@
     loop(nt, send_back)
     bar[t] = bas[...]
 
+    if far > 3:
+        ring_step(3)
     if far > 4:
         ring_step(4)
     wait_in(hbuf.at[1 - yl], h_recv)

time: 106 us -> 104 us (0.981)
  the two profiles are of different devices: /device:TPU:8 before, /device:TPU:81 now
where the time goes in v5:
time: 104 us; the launch traced here: 103 us
  Pallas kernels  103 us (99%)
    pallas_call x1, Pallas kernels, per_device(): pl.pallas_call(functools.partial(kernel, nt=nt, nz=nz), out_shape=(jax.Sh...  100 us
    pallas_call x1, Pallas kernels, per_device(): pl.pallas_call(hand_over, out_shape=[jax.ShapeDtypeStruct(r.shape, r.dtyp...  2.31 us

profile of v5, /device:TPU:81, one launch (start us, length us, event | category | flops | bytes accessed | tf_op | source)
XLA Modules:
  0.0 103.4 jit_solution(5957590044086209747)
XLA Ops:
  0.6 100.4 %dora.1 = (bf16[256,256]{1,0:T(8,128)(2,1)}, bf16[256,896]{1,0:T(8,128)(2,1)}, f32[896,128]{1,0:T(8,128)}, f32[128,256]{1,0:T(8,128)}, f32[4,256]{1,0:T(4,128)}) custom-call(bf16[256,896]{1,0:T(8,128)(2,1)} %h_hbm.1, s32[16]{0:T(128)} %tid.1, bf16[896,128]{1,0:T(8,128)(2,1)} %w_hbm.1, bf16[896,128]{1,0:T(8,128)(2,1)} %a_hbm.1, bf16[128,256]{1,0:T(8,128)(2,1)} %o_hbm.1, ...), custom_call_target="tpu_custom_call" | custom-call | tf_op jit(solution)/shard_map/dora/pallas_call | solution.py:589
  101.0 2.3 %hand_over.1 = (bf16[256,256]{1,0:T(8,128)(2,1)}, bf16[256,896]{1,0:T(8,128)(2,1)}, f32[896,128]{1,0:T(8,128)}, f32[128,256]{1,0:T(8,128)}, f32[4,256]{1,0:T(4,128)}) custom-call(bf16[256,256]{1,0:T(8,128)(2,1)} %get-tuple-element.10.refs_0_, bf16[256,896]{1,0:T(8,128)(2,1)} %get-tuple-element.11.refs_1_, f32[896,128]{1,0:T(8,128)} %get-tuple-element.12.refs_2_, ...), custom_call_target="tpu_custom_call" | custom-call | tf_op jit(solution)/shard_map/hand_over/pallas_call | solution.py:606

commit v6 on v5

--- a/solution.py
+++ b/solution.py
@@ -180,8 +180,8 @@
     def _():
         sqr[t] = sqs[...]
 
+    remote(hbuf.at[yl], hbuf.at[yl], h_send, h_recv, pair, t).start()
     ring_step(1)
-    remote(hbuf.at[yl], hbuf.at[yl], h_send, h_recv, pair, t).start()
 
     @pl.when(t == lead)
     def _():

time: 104 us -> 101 us (0.971)
  the two profiles are of different devices: /device:TPU:81 before, /device:TPU:17 now
where the time goes in v6:
time: 101 us
  Pallas kernels  100 us (99%)
    pallas_call x1, Pallas kernels, per_device(): pl.pallas_call(functools.partial(kernel, nt=nt, nz=nz), out_shape=(jax.Sh...  97.8 us
    pallas_call x1, Pallas kernels, per_device(): pl.pallas_call(hand_over, out_shape=[jax.ShapeDtypeStruct(r.shape, r.dtyp...  2.31 us

profile of v6, /device:TPU:17, one launch (start us, length us, event | category | flops | bytes accessed | tf_op | source)
XLA Modules:
  0.0 100.8 jit_solution(7322770021012158437)
XLA Ops:
  0.6 97.8 %dora.1 = (bf16[256,256]{1,0:T(8,128)(2,1)}, bf16[256,896]{1,0:T(8,128)(2,1)}, f32[896,128]{1,0:T(8,128)}, f32[128,256]{1,0:T(8,128)}, f32[4,256]{1,0:T(4,128)}) custom-call(bf16[256,896]{1,0:T(8,128)(2,1)} %h_hbm.1, s32[16]{0:T(128)} %tid.1, bf16[896,128]{1,0:T(8,128)(2,1)} %w_hbm.1, bf16[896,128]{1,0:T(8,128)(2,1)} %a_hbm.1, bf16[128,256]{1,0:T(8,128)(2,1)} %o_hbm.1, ...), custom_call_target="tpu_custom_call" | custom-call | tf_op jit(solution)/shard_map/dora/pallas_call | solution.py:589
  98.5 2.3 %hand_over.1 = (bf16[256,256]{1,0:T(8,128)(2,1)}, bf16[256,896]{1,0:T(8,128)(2,1)}, f32[896,128]{1,0:T(8,128)}, f32[128,256]{1,0:T(8,128)}, f32[4,256]{1,0:T(4,128)}) custom-call(bf16[256,256]{1,0:T(8,128)(2,1)} %get-tuple-element.10.refs_0_, bf16[256,896]{1,0:T(8,128)(2,1)} %get-tuple-element.11.refs_1_, f32[896,128]{1,0:T(8,128)} %get-tuple-element.12.refs_2_, ...), custom_call_target="tpu_custom_call" | custom-call | tf_op jit(solution)/shard_map/hand_over/pallas_call | solution.py:606
